TPU v7x, 256 devices: a whole 4x4x8 slice. The times are simulated.
256 devices in a mesh: src: 32 (over y, x, core), tgt: 8 (over z).
Axes of the slice: x: 4, y: 4, z: 8, core: 2. Of those that a mesh axis runs over, the one named last changes fastest.
Arguments:
- src_points: bfloat16 [32, 524288], P(None, 'src'), may hold values from -24 to 24
- tgt_points: bfloat16 [32, 524288], P(None, 'tgt'), may hold values from -6 to 6
- tgt_potential: float32 [524288], P('tgt'), may hold values from -2 to 2
- support: int32 [4096, 8, 6], P('src', 'tgt'), may hold values from 0 to 511, as said below
- counts: int32 [4096, 8], P('src', 'tgt'), may hold values from 1 to 6, as said below
Outputs:
- src_potential: float32 [524288], P('src')
- new_tgt_potential: float32 [524288], P('tgt')
Inputs may be any that keep to these rules, and one draw needn't show every extreme that they name: support[r, t, k] names target block t * 512 + support[r, t, k]; the first counts[r, t] entries of a list are distinct; every target block is named in the used part of some list. `counts`: for every source block the list of some target shard is full.
All inputs are finite; a program needn't handle non-finite values.
Results may differ from a plain program's by a relative error of at most 0.0004.
Values sent between devices are 32-bit elements; how exact they have to be, the bound alone decides.
A program may use at most 128 MiB of HBM per device.

v0:
```python
import math
import jax
import jax.numpy as jnp
from jax import lax
from jax.sharding import PartitionSpec as P

BLK = 128
entropy_blur = 0.05
neg_fill = -1e30


def body(src_points, tgt_points, tgt_potential, support, counts):
    features = src_points.shape[0]
    src_count = src_points.shape[1]
    tgt_count = tgt_points.shape[1]
    src_blocks = src_count // BLK
    tgt_blocks = tgt_count // BLK
    slot_count = support.shape[2]
    total_src = src_count * lax.axis_size("src")
    total_tgt = tgt_count * lax.axis_size("tgt")
    per_step = math.gcd(src_blocks, 8)
    step_count = src_blocks // per_step
    block_lists = support[:, 0, :]
    live_slots = jnp.arange(slot_count, dtype=jnp.int32)[None, :] < counts[:, 0][:, None]
    src_sq = jnp.sum(jnp.square(src_points.astype(jnp.float32)), axis=0).reshape(src_blocks, BLK)
    tgt_cube = tgt_points.reshape(features, tgt_blocks, BLK)
    tgt_sq = jnp.sum(jnp.square(tgt_points.astype(jnp.float32)), axis=0).reshape(tgt_blocks, BLK)
    tgt_pot = tgt_potential.reshape(tgt_blocks, BLK)

    def group_cost(step_index):
        first_block = step_index * per_step
        src_rows = lax.dynamic_slice_in_dim(src_points, first_block * BLK, per_step * BLK, 1)
        src_rows = src_rows.reshape(features, per_step, BLK)
        picked = lax.dynamic_slice_in_dim(block_lists, first_block, per_step, 0)
        live_mask = lax.dynamic_slice_in_dim(live_slots, first_block, per_step, 0)
        rows_sq = lax.dynamic_slice_in_dim(src_sq, first_block, per_step, 0)
        near_points = jnp.take(tgt_cube, picked.reshape(-1), axis=1).reshape(
            features, per_step, slot_count, BLK
        )
        inner_prod = jnp.einsum(
            "dgi,dgkj->gikj", src_rows, near_points, preferred_element_type=jnp.float32
        )
        cost_tile = (rows_sq[:, :, None, None] + tgt_sq[picked][:, None, :, :]) / (
            2.0 * features
        ) - inner_prod / features
        return (cost_tile, picked, live_mask)

    def row_part(step_index):
        cost_tile, picked, live_mask = group_cost(step_index)
        row_score = jnp.where(
            live_mask[:, None, :, None],
            (tgt_pot[picked][:, None, :, :] - cost_tile) / entropy_blur,
            neg_fill,
        )
        highest = jnp.max(row_score, axis=(2, 3))
        summed = jnp.sum(jnp.exp(row_score - highest[:, :, None, None]), axis=(2, 3))
        return (highest, summed)

    row_high, row_total = lax.map(row_part, jnp.arange(step_count, dtype=jnp.int32))
    row_high = row_high.reshape(src_count)
    row_total = row_total.reshape(src_count)
    global_high = lax.pmax(row_high, "tgt")
    row_total = lax.psum(row_total * jnp.exp(row_high - global_high), "tgt")
    row_high = global_high
    src_potential = -entropy_blur * (row_high + jnp.log(row_total) - math.log(total_tgt))
    src_pot = src_potential.reshape(src_blocks, BLK)

    def col_part(step_index):
        cost_tile, picked, live_mask = group_cost(step_index)
        block_pot = lax.dynamic_slice_in_dim(src_pot, step_index * per_step, per_step, 0)
        col_score = jnp.where(
            live_mask[:, None, :, None],
            (block_pot[:, :, None, None] - cost_tile) / entropy_blur,
            neg_fill,
        )
        highest = jnp.max(col_score, axis=1)
        summed = jnp.sum(jnp.exp(col_score - highest[:, None]), axis=1)
        return (highest, summed)

    tile_high, tile_total = lax.map(col_part, jnp.arange(step_count, dtype=jnp.int32))
    tile_high = tile_high.reshape(src_blocks * slot_count, BLK)
    tile_total = tile_total.reshape(src_blocks * slot_count, BLK)
    owners = jnp.where(live_slots, block_lists, tgt_blocks).reshape(-1)
    seg_high = jax.ops.segment_max(tile_high, owners, num_segments=tgt_blocks + 1)
    seg_total = jax.ops.segment_sum(
        tile_total * jnp.exp(tile_high - seg_high[owners]), owners, num_segments=tgt_blocks + 1
    )
    col_high = jnp.maximum(seg_high[:tgt_blocks], neg_fill).reshape(tgt_count)
    col_total = seg_total[:tgt_blocks].reshape(tgt_count)
    global_high = lax.pmax(col_high, "src")
    global_total = lax.psum(col_total * jnp.exp(col_high - global_high), "src")
    new_tgt_potential = -entropy_blur * (global_high + jnp.log(global_total) - math.log(total_src))
    return (src_potential, new_tgt_potential)


def solution(mesh):
    return jax.shard_map(
        body,
        mesh=mesh,
        in_specs=(P(None, "src"), P(None, "tgt"), P("tgt"), P("src", "tgt", None), P("src", "tgt")),
        out_specs=(P("src"), P("tgt")),
        check_vma=False,
    )
```

profile of v0, /device:TPU:1, one launch (start us, length us, event | category | flops | bytes accessed | tf_op | source)
XLA Modules:
  0.0 693.1 jit_solution(16128332528436720844)
XLA Ops:
  7.2 5.0 copy_bitcast_fusion
  14.0 156.2 %while.28 = (s32[]{:T(128)}, f32[16,8,128]{2,1,0:T(8,128)S(1)}, f32[16,8,128]{2,1,0:T(8,128)S(1)}, s32[16]{0:T(128)S(1)}, pred[128,6]{1,0:T(8,128)(4,1)S(1)}, /*...) while((s32[]{:T(128)}, f32[16,8,128]{2,1,0:T(8,128)S(1)}, ...), condition=%wide.region_5.7_spmd, body=%wide.region_2.6_spmd.sunk | while | flops 58393160 | bytes 8883529 | solution.py:59
  15.4 2.8 gather_fusion
  20.4 3.0 fusion.24
  25.2 2.8 gather_fusion
  30.1 3.0 fusion.24
  39.9 3.0 fusion.24
  44.7 2.8 gather_fusion
  49.7 3.0 fusion.24
  54.5 2.8 gather_fusion
  59.4 3.0 fusion.24
  64.2 2.8 gather_fusion
  69.2 3.0 fusion.24
  74.0 2.8 gather_fusion
  79.0 3.0 fusion.24
  83.7 2.8 gather_fusion
  88.7 3.0 fusion.24
  98.5 3.0 fusion.24
  108.2 3.0 fusion.24
  118.0 3.0 fusion.24
  127.8 3.0 fusion.24
  137.5 3.0 fusion.24
  147.3 3.0 fusion.24
  157.0 3.0 fusion.24
  166.8 3.0 fusion.24
  171.3 70.0 %all-reduce.5.cloned.1.call-done = f32[16384]{0:T(1024)} async-done(((f32[16384]{0:T(1024)}), f32[16384]{0:T(1024)}) %all-reduce.5.cloned.1.call-update) | async-done | bytes 65552 | tf_op jit(solution)/shard_map/pmax | solution.py:62
  242.8 71.3 %all-reduce.7.cloned.1.call-done = f32[16384]{0:T(1024)} async-done(((f32[16384]{0:T(1024)}), f32[16384]{0:T(1024)}) %all-reduce.7.cloned.1.call-update) | async-done | bytes 65552 | tf_op jit(solution)/shard_map/psum | solution.py:63
  315.0 133.0 %while.29 = (s32[]{:T(128)}, f32[16,8,6,128]{3,2,1,0:T(8,128)S(1)}, f32[16,8,6,128]{3,2,1,0:T(8,128)S(1)}, s32[16]{0:T(128)S(1)}, pred[128,6]{1,0:T(8,128)(4,1)S...) while((s32[]{:T(128)}, f32[16,8,6,128]{3,2,1,0:T(8,128)S(1)}, ...), condition=%wide.region_11.13_spmd, body=%wide.region_8.12_spmd.sunk | while | flops 58382920 | bytes 8948877 | solution.py:80
  448.1 6.1 scatter_custom_fusion
  455.2 9.2 %scatter_custom_fusion.1 = f32[513,128]{1,0:T(8,128)S(1)} fusion(s32[768]{0:T(1024)S(1)} %get-tuple-element.306, f32[768,128]{1,0:T(8,128)S(1)} %reshape.162, f32[768,128]{1,0:T(8,128)S(1)} %reshape.216, f32[]{:T(128)} %constant.183.clone.1, f32[513,128]{1,0:T(8,128)S(1)} %scatter_custom_fusion, s32[1024]{0:T(1024)S(1)} %pad_clamp_fusion.4), kind=kCustom, calls=%fused_computation.42 | custom fusion | flops 294912 | bytes 1319428 | tf_op jit(solution)/shard_map/scatter-add | solution.py:85
  464.4 105.5 %all-reduce.9.cloned.1.call-done = f32[65536]{0:T(1024)} async-done(((f32[65536]{0:T(1024)}), f32[65536]{0:T(1024)}) %all-reduce.9.cloned.1.call-update) | async-done | bytes 262160 | tf_op jit(solution)/shard_map/pmax | solution.py:90
  571.7 113.1 %all-reduce.11.cloned.1.call-done = f32[65536]{0:T(1024)} async-done(((f32[65536]{0:T(1024)}), f32[65536]{0:T(1024)}) %all-reduce.11.cloned.1.call-update) | async-done | bytes 262160 | tf_op jit(solution)/shard_map/psum | solution.py:91
  (676 shorter events, 186.7 us)
Async XLA Ops:
  7.2 234.0 %all-reduce.5.cloned.1.call-start = ((), (), s32[]{:S(2)}) async-start(), calls=%async_computation | async-start | bytes 131072 | tf_op jit(solution)/shard_map/pmax | solution.py:62
  7.2 5.0 copy-start
  12.2 1.3 copy-start.5
  12.2 1.4 copy-start.6
  12.2 1.5 copy-start.2
  12.2 1.8 copy-start.1
  170.2 0.6 copy-start.3
  170.9 143.2 %all-reduce.7.cloned.1.call-start = ((), (), s32[]{:S(2)}) async-start(), calls=%async_computation.1 | async-start | bytes 131072 | tf_op jit(solution)/shard_map/psum | solution.py:63
  242.8 327.2 %all-reduce.9.cloned.1.call-start = ((), (), s32[]{:S(2)}) async-start(), calls=%async_computation.2 | async-start | bytes 524288 | tf_op jit(solution)/shard_map/pmax | solution.py:90
  448.0 238.6 %copy-start.4 = (f32[128,128]{1,0:T(8,128)}, f32[128,128]{1,0:T(8,128)S(1)}, u32[]{:S(2)}) copy-start(f32[128,128]{1,0:T(8,128)S(1)} %get-tuple-element.643) | copy-start | bytes 196612
  454.9 229.9 %all-reduce.11.cloned.1.call-start = ((), (), s32[]{:S(2)}) async-start(), calls=%async_computation.3 | async-start | bytes 524288 | tf_op jit(solution)/shard_map/psum | solution.py:91
Sparse Core Ops, SparseCore 0:
  171.0 70.1 all-reduce.4
  244.2 69.8 all-reduce.6
  455.0 114.8 all-reduce.8
  573.6 111.1 all-reduce.10
where the time goes:
time: 695 us; the launch traced here: 693 us
  waiting for transfers between devices  360 us (52%)
  local copies, waits for them, and re-layouts  150 us (22%)
  matrix products  76.1 us (11%)
  other arithmetic  47.1 us (7%)
  loops' own time  45.3 us (7%)
  between operations  14 us (2%)
    psum x1, waiting for transfers between devices, body(): global_total = lax.psum(col_total * jnp.exp(col_high - global_high), 'src')  113 us
    pmax x1, waiting for transfers between devices, body(): global_high = lax.pmax(col_high, 'src')  106 us
    gather x32, local copies, waits for them, and re-layouts, group_cost(): jnp.take(tgt_cube, picked.reshape(-1), axis=1)  90 us
    dot_general x32, matrix products, group_cost(): jnp.einsum('dgi,dgkj->gikj', src_rows, near_points, preferred_element_typ...  76.1 us
    psum x1, waiting for transfers between devices, body(): row_total = lax.psum(row_total * jnp.exp(row_high - global_high), 'tgt')  71.3 us
    pmax x1, waiting for transfers between devices, body(): global_high = lax.pmax(row_high, 'tgt')  70 us
    another operation x1, loops' own time, body(): lax.map(col_part, jnp.arange(step_count, dtype=jnp.int32))  22.7 us
    another operation x1, loops' own time, body(): lax.map(row_part, jnp.arange(step_count, dtype=jnp.int32))  22.6 us
  transfers between devices with their start and end apart: 4, of which 4 were waited for; matrix products, arithmetic and copies ran while one was open for 1% of the time, Pallas kernels for 0%

commit v1 on v0

--- a/solution.py
+++ b/solution.py
@@ -1,3 +1,4 @@
+import functools
 import math
 import jax
 import jax.numpy as jnp
@@ -7,6 +8,13 @@
 BLK = 128
 entropy_blur = 0.05
 neg_fill = -1e30
+
+
+def point_grid(t0, axis_tag):
+    return jnp.sum(lax.all_gather(t0, axis_tag), axis=0)
+
+
+direct_links = functools.partial(point_grid, axis_tag="src")
 
 
 def body(src_points, tgt_points, tgt_potential, support, counts):
@@ -88,7 +96,7 @@
     col_high = jnp.maximum(seg_high[:tgt_blocks], neg_fill).reshape(tgt_count)
     col_total = seg_total[:tgt_blocks].reshape(tgt_count)
     global_high = lax.pmax(col_high, "src")
-    global_total = lax.psum(col_total * jnp.exp(col_high - global_high), "src")
+    global_total = direct_links(col_total * jnp.exp(col_high - global_high))
     new_tgt_potential = -entropy_blur * (global_high + jnp.log(global_total) - math.log(total_src))
     return (src_potential, new_tgt_potential)
 

time: 695 us -> 652 us (0.938)
  waiting for transfers between devices: 360 us -> 306 us
    psum x1 -> x0, waiting for transfers between devices: 113 us -> none  [body(): global_total = lax.psum(col_total * jnp.exp(col_high - global_high), 'src')]
    all_gather x0 -> x1, waiting for transfers between devices: none -> 59.5 us  [point_grid(): return jnp.sum(lax.all_gather(t0, axis_tag), axis=0)]
    all_gather x0 -> x1, local copies, waits for them, and re-layouts: none -> 7.47 us  [point_grid(): return jnp.sum(lax.all_gather(t0, axis_tag), axis=0)]
where the time goes in v1:
time: 652 us; the launch traced here: 650 us
  waiting for transfers between devices  306 us (47%)
  local copies, waits for them, and re-layouts  156 us (24%)
  matrix products  76 us (12%)
  other arithmetic  52.7 us (8%)
  loops' own time  45.4 us (7%)
  between operations  14 us (2%)
    pmax x1, waiting for transfers between devices, body(): global_high = lax.pmax(col_high, 'src')  106 us
    gather x32, local copies, waits for them, and re-layouts, group_cost(): jnp.take(tgt_cube, picked.reshape(-1), axis=1)  90 us
    dot_general x32, matrix products, group_cost(): jnp.einsum('dgi,dgkj->gikj', src_rows, near_points, preferred_element_typ...  76 us
    psum x1, waiting for transfers between devices, body(): row_total = lax.psum(row_total * jnp.exp(row_high - global_high), 'tgt')  71.3 us
    pmax x1, waiting for transfers between devices, body(): global_high = lax.pmax(row_high, 'tgt')  70 us
    all_gather x1, waiting for transfers between devices, point_grid(): return jnp.sum(lax.all_gather(t0, axis_tag), axis=0)  59.5 us
    another operation x1, loops' own time, body(): lax.map(col_part, jnp.arange(step_count, dtype=jnp.int32))  22.7 us
    another operation x1, loops' own time, body(): lax.map(row_part, jnp.arange(step_count, dtype=jnp.int32))  22.7 us
  transfers between devices with their start and end apart: 4, of which 4 were waited for; matrix products, arithmetic and copies ran while one was open for 1% of the time, Pallas kernels for 0%

profile of v1, /device:TPU:1, one launch (start us, length us, event | category | flops | bytes accessed | tf_op | source)
XLA Modules:
  0.0 650.2 jit_solution(9754515273704020955)
XLA Ops:
  7.2 3.6 multiply_reduce_fusion
  14.1 156.2 %while.28 = (s32[]{:T(128)}, f32[16,8,128]{2,1,0:T(8,128)S(1)}, f32[16,8,128]{2,1,0:T(8,128)S(1)}, s32[16]{0:T(128)S(1)}, pred[128,6]{1,0:T(8,128)(4,1)S(1)}, /*...) while((s32[]{:T(128)}, f32[16,8,128]{2,1,0:T(8,128)S(1)}, ...), condition=%wide.region_5.7_spmd, body=%wide.region_2.6_spmd.sunk | while | flops 58393160 | bytes 8883537 | solution.py:67
  17.5 2.8 gather_fusion
  20.4 3.0 fusion.24
  30.2 3.0 fusion.24
  39.9 3.0 fusion.24
  49.7 3.0 fusion.24
  56.5 2.8 gather_fusion
  59.5 3.0 fusion.24
  69.2 3.0 fusion.24
  79.0 3.0 fusion.24
  88.7 3.0 fusion.24
  95.5 2.8 gather_fusion
  98.5 3.0 fusion.24
  108.3 3.0 fusion.24
  115.1 2.8 gather_fusion
  118.0 3.0 fusion.24
  127.8 3.0 fusion.24
  134.6 2.8 gather_fusion
  137.5 3.0 fusion.24
  147.3 3.0 fusion.24
  157.1 3.0 fusion.24
  166.8 3.0 fusion.24
  171.3 70.0 %all-reduce.4.cloned.1.call-done = f32[16384]{0:T(1024)} async-done(((f32[16384]{0:T(1024)}), f32[16384]{0:T(1024)}) %all-reduce.4.cloned.1.call-update) | async-done | bytes 65552 | tf_op jit(solution)/shard_map/pmax | solution.py:70
  242.8 71.3 %all-reduce.6.cloned.1.call-done = f32[16384]{0:T(1024)} async-done(((f32[16384]{0:T(1024)}), f32[16384]{0:T(1024)}) %all-reduce.6.cloned.1.call-update) | async-done | bytes 65552 | tf_op jit(solution)/shard_map/psum | solution.py:71
  315.0 133.0 %while.29 = (s32[]{:T(128)}, f32[16,8,6,128]{3,2,1,0:T(8,128)S(1)}, f32[16,8,6,128]{3,2,1,0:T(8,128)S(1)}, s32[16]{0:T(128)S(1)}, pred[128,6]{1,0:T(8,128)(4,1)S...) while((s32[]{:T(128)}, f32[16,8,6,128]{3,2,1,0:T(8,128)S(1)}, ...), condition=%wide.region_11.13_spmd, body=%wide.region_8.12_spmd.sunk | while | flops 58382920 | bytes 8948885 | solution.py:88
  448.1 6.1 scatter_custom_fusion
  455.2 9.2 %scatter_custom_fusion.1 = f32[513,128]{1,0:T(8,128)S(1)} fusion(s32[768]{0:T(1024)S(1)} %get-tuple-element.350, f32[768,128]{1,0:T(8,128)S(1)} %reshape.162, f32[768,128]{1,0:T(8,128)S(1)} %reshape.216, f32[]{:T(128)} %constant.183.clone.1, f32[513,128]{1,0:T(8,128)S(1)} %scatter_custom_fusion, s32[1024]{0:T(1024)S(1)} %pad_clamp_fusion.4), kind=kCustom, calls=%fused_computation.42 | custom fusion | flops 294912 | bytes 1319428 | tf_op jit(solution)/shard_map/scatter-add | solution.py:93
  464.4 105.5 %all-reduce.8.cloned.1.call-done = f32[65536]{0:T(1024)} async-done(((f32[65536]{0:T(1024)}), f32[65536]{0:T(1024)}) %all-reduce.8.cloned.1.call-update) | async-done | bytes 262160 | tf_op jit(solution)/shard_map/pmax | solution.py:98
  571.6 59.5 %all-gather.3.cloned.1.call-done = f32[2097152]{0:T(1024)} async-done(((f32[65536]{0:T(1024)}), f32[2097152]{0:T(1024)}) %all-gather.3.cloned.1.call-update) | async-done | bytes 8388624 | tf_op jit(solution)/shard_map/all_gather | solution.py:14
  631.1 7.5 %reshape.228 = f32[32,65536]{1,0:T(8,128)} reshape(f32[2097152]{0:T(1024)} %all-gather.3.cloned.1.call-done) | data formatting | bytes 16777216 | tf_op jit(solution)/shard_map/all_gather | solution.py:14
  638.6 4.3 reduce_sum.53
  (680 shorter events, 192.6 us)
Async XLA Ops:
  7.2 234.1 %all-reduce.4.cloned.1.call-start = ((), (), s32[]{:S(2)}) async-start(), calls=%async_computation | async-start | bytes 131072 | tf_op jit(solution)/shard_map/pmax | solution.py:70
  7.2 3.6 copy-start
  10.8 2.7 copy-start.7
  10.8 2.8 copy-start.6
  10.8 2.9 copy-start.2
  10.9 3.2 copy-start.1
  170.2 0.6 copy-start.4
  170.9 143.2 %all-reduce.6.cloned.1.call-start = ((), (), s32[]{:S(2)}) async-start(), calls=%async_computation.1 | async-start | bytes 131072 | tf_op jit(solution)/shard_map/psum | solution.py:71
  242.8 327.1 %all-reduce.8.cloned.1.call-start = ((), (), s32[]{:S(2)}) async-start(), calls=%async_computation.2 | async-start | bytes 524288 | tf_op jit(solution)/shard_map/pmax | solution.py:98
  448.0 190.6 %copy-start.5 = (f32[128,128]{1,0:T(8,128)}, f32[128,128]{1,0:T(8,128)S(1)}, u32[]{:S(2)}) copy-start(f32[128,128]{1,0:T(8,128)S(1)} %get-tuple-element.687) | copy-start | bytes 196612
  454.9 176.2 %all-gather.3.cloned.1.call-start = ((), (), s32[]{:S(2)}) async-start(), calls=%async_computation.3 | async-start | bytes 8650752 | tf_op jit(solution)/shard_map/all_gather | solution.py:14
  638.6 4.3 copy-start.3
Sparse Core Ops, SparseCore 0:
  171.0 70.1 all-reduce.3
  244.2 69.8 all-reduce.5
  455.0 114.8 all-reduce.7
  572.9 58.1 all-gather.2
